TPU v7x, 512 devices: a whole 4x4x16 slice. The times are simulated.
512 devices in a mesh: dp: 16 (over y, x), mp: 32 (over z, core).
Axes of the slice: x: 4, y: 4, z: 16, core: 2. Of those that a mesh axis runs over, the one named last changes fastest.
Arguments:
- temporal: bfloat16 [16384, 4096], P('dp', 'mp'), may hold values from -6 to 6
- code_ids: int32 [16384, 7], P('dp'), may hold values from 0 to 2047
- context_weight: bfloat16 [4096, 1024], P('mp'), may hold values from -0.09375 to 0.09375
- code_tables: bfloat16 [7, 2048, 1024], P(None, None, 'mp'), may hold values from -6 to 6
- gate_proj: bfloat16 [1024, 1536], P(None, 'mp'), may hold values from -0.1875 to 0.1875
- up_proj: bfloat16 [1024, 1536], P(None, 'mp'), may hold values from -0.1875 to 0.1875
- down_proj: bfloat16 [1536, 1024], P('mp'), may hold values from -0.15625 to 0.15625
- out_grad: bfloat16 [16384, 8, 1024], P(('dp', 'mp')), may hold values from -6 to 6
Outputs:
- depth_out: bfloat16 [16384, 8, 1024], P(('dp', 'mp'))
- temporal_grad: bfloat16 [16384, 4096], P('dp', 'mp')
- context_grad: float32 [4096, 1024], P('mp', 'dp')
All inputs are finite; a program needn't handle non-finite values.
Results may differ from a plain program's by a relative error of at most 0.025.
Values may be sent and summed in bfloat16 or wider, within the bound.
A program may use at most 64 MiB of HBM per device.

v0:
```python
import jax
import jax.numpy as jnp
from jax import lax
from jax.sharding import PartitionSpec as P


def contract_last(left, right):
    return lax.dot_general(
        left, right, (((1,), (1,)), ((), ())), preferred_element_type=jnp.float32
    )


def contract_first(left, right):
    return lax.dot_general(
        left, right, (((0,), (0,)), ((), ())), preferred_element_type=jnp.float32
    )


def depth_forward(inputs, weights):
    gate_proj, up_proj, down_proj = weights
    meansq = jnp.mean(inputs * inputs, axis=-1, keepdims=True)
    inv_rms = lax.rsqrt(meansq + 1e-06)
    normed = inputs * inv_rms
    normed_low = normed.astype(jnp.bfloat16)
    gate_act = jnp.dot(normed_low, gate_proj, preferred_element_type=jnp.float32)
    upper = jnp.dot(normed_low, up_proj, preferred_element_type=jnp.float32)
    sigmoid_gate = jax.nn.sigmoid(gate_act)
    hidden = (gate_act * sigmoid_gate * upper).astype(jnp.bfloat16)
    branch = jnp.dot(hidden, down_proj, preferred_element_type=jnp.float32)
    output = (inputs + branch).astype(jnp.bfloat16)
    return (output, (normed, inv_rms, gate_act, upper, sigmoid_gate))


def depth_backward(out_grad, saved, weights):
    gate_proj, up_proj, down_proj = weights
    normed, inv_rms, gate_act, upper, sigmoid_gate = saved
    hidden_grad = contract_last(out_grad, down_proj)
    gate_grad = (
        hidden_grad * upper * sigmoid_gate * (1.0 + gate_act * (1.0 - sigmoid_gate))
    ).astype(jnp.bfloat16)
    up_grad = (hidden_grad * gate_act * sigmoid_gate).astype(jnp.bfloat16)
    normed_grad = contract_last(gate_grad, gate_proj) + contract_last(up_grad, up_proj)
    return out_grad.astype(jnp.float32) + inv_rms * (
        normed_grad - normed * jnp.mean(normed_grad * normed, axis=-1, keepdims=True)
    )


def per_device(
    temporal, code_ids, context_weight, code_tables, gate_proj, up_proj, down_proj, out_grad
):
    groups = lax.axis_size("mp")
    steps_dev = out_grad.shape[0]
    levels = out_grad.shape[1]
    model_width = out_grad.shape[2]
    inputs_levels = code_tables.shape[0]
    flat_tables = code_tables.reshape(inputs_levels * code_tables.shape[1], code_tables.shape[2])
    offsets = jnp.arange(inputs_levels, dtype=jnp.int32) * code_tables.shape[1]
    looked = flat_tables[code_ids + offsets[None, :]]
    looked = looked.reshape(groups, steps_dev, inputs_levels, code_tables.shape[2])
    context = lax.psum_scatter(
        jnp.dot(temporal, context_weight, preferred_element_type=jnp.float32).astype(jnp.bfloat16),
        "mp",
        scatter_dimension=0,
        tiled=True,
    ).astype(jnp.float32)
    embedded = lax.all_to_all(looked, "mp", split_axis=0, concat_axis=3, tiled=True)
    embedded = embedded.reshape(steps_dev, inputs_levels, model_width)
    leading = jnp.zeros((steps_dev, 1, model_width), jnp.bfloat16)
    inputs = jnp.concatenate([leading, embedded], axis=1).astype(jnp.float32) + context[:, None, :]
    gathered = (
        lax.all_gather(gate_proj, "mp", axis=1, tiled=True),
        lax.all_gather(up_proj, "mp", axis=1, tiled=True),
        lax.all_gather(down_proj, "mp", axis=0, tiled=True),
    )
    output, saved = depth_forward(inputs.reshape(steps_dev * levels, model_width), gathered)
    input_grad = depth_backward(out_grad.reshape(steps_dev * levels, model_width), saved, gathered)
    context_back = jnp.sum(input_grad.reshape(steps_dev, levels, model_width), axis=1).astype(
        jnp.bfloat16
    )
    gathered_grad = lax.all_gather(context_back, "mp", axis=0, tiled=True)
    temporal_grad = contract_last(gathered_grad, context_weight).astype(jnp.bfloat16)
    grad_term = contract_first(temporal, gathered_grad) / gathered_grad.shape[0]
    context_grad = lax.psum_scatter(
        grad_term.astype(jnp.bfloat16), "dp", scatter_dimension=1, tiled=True
    ).astype(jnp.float32)
    return (output.reshape(steps_dev, levels, model_width), temporal_grad, context_grad)


def solution(mesh):
    in_specs = (
        P("dp", "mp"),
        P("dp", None),
        P("mp", None),
        P(None, None, "mp"),
        P(None, "mp"),
        P(None, "mp"),
        P("mp", None),
        P(("dp", "mp"), None, None),
    )
    out_specs = (P(("dp", "mp"), None, None), P("dp", "mp"), P("mp", "dp"))
    return jax.shard_map(
        per_device, mesh=mesh, in_specs=in_specs, out_specs=out_specs, check_vma=False
    )
```

profile of v0, /device:TPU:1, one launch (start us, length us, event | category | flops | bytes accessed | tf_op | source)
XLA Modules:
  0.0 527.1 jit_solution(7191996263923353074)
XLA Ops:
  7.2 0.0 reduce-scatter.3.cloned.1.call-start
  7.2 0.9 copy-done
  8.1 2.9 convolution_convert_fusion
  11.1 0.0 reduce-scatter.3.cloned.1.call-update
  11.1 0.0 all-gather.7.cloned.1.call-start
  11.1 0.7 all-gather.7.cloned.1.call-update
  11.8 0.0 all-gather.5.cloned.1.call-start
  11.9 0.7 all-gather.5.cloned.1.call-update
  12.6 0.0 all-gather.9.cloned.1.call-start
  12.6 0.5 all-gather.9.cloned.1.call-update
  13.2 0.0 all-gather.11.cloned.1.call-start
  13.2 3.0 copy.17
  16.2 0.1 compare_select_fusion
  16.2 0.2 copy.18
  16.5 0.3 reshape.63
  16.9 21.7 %gather_fusion = bf16[7168,32]{1,0:T(8,128)(2,1)S(1)} fusion(bf16[14336,32]{1,0:T(8,128)(2,1)} %bitcast.47, s32[7168]{0:T(1024)S(1)} %broadcast_clamp_fusion), kind=kCustom, calls=%fused_computation | custom fusion | bytes 946176 | tf_op jit(solution)/shard_map/gather | solution.py:58
  38.5 1.7 reshape.55
  40.3 1.9 copy.34
  42.2 1.3 reshape.72
  43.6 46.4 %all_to_all.15 = bf16[32,2,3584]{2,1,0:T(2,128)(2,1)S(1)} all-to-all(bf16[32,2,3584]{2,1,0:T(2,128)(2,1)S(1)} %reshape.72), channel_id=1, replica_groups=mesh['dp'=16,'mp'=32] {'mp'}, dimensions={0} | all-to-all | bytes 917504 | tf_op jit(solution)/shard_map/all_to_all | solution.py:66
  90.0 1.0 reshape.73
  91.0 0.3 bitcast_bitcast_fusion
  91.4 0.7 copy.20
  92.1 2.0 reshape.56
  94.0 37.8 %reduce-scatter.3.cloned.1.call-done = bf16[32,1024]{1,0:T(8,128)(2,1)} async-done(((bf16[1024,1024]{1,0:T(8,128)(2,1)}), bf16[32,1024]{1,0:T(8,128)(2,1)}) %reduce-scatter.3.cloned.1.call-update) | async-done | bytes 65552 | tf_op jit(solution)/shard_map/reduce_scatter | solution.py:60
  131.8 0.8 convert_element_type.44
  132.7 0.2 multiply_reduce_fusion.1
  132.9 0.1 copy.22
  133.0 0.1 rsqrt.12
  133.1 76.8 %all-gather.7.cloned.1.call-done = bf16[1024,1536]{0,1:T(8,128)(2,1)} async-done(((bf16[1024,48]{0,1:T(8,128)(2,1)}), bf16[1024,1536]{0,1:T(8,128)(2,1)}) %all-gather.7.cloned.1.call-update) | async-done | bytes 3145744 | tf_op jit(solution)/shard_map/all_gather | solution.py:72
  209.8 3.3 fusion.13
  213.1 69.2 %all-gather.5.cloned.1.call-done = bf16[1024,1536]{0,1:T(8,128)(2,1)} async-done(((bf16[1024,48]{0,1:T(8,128)(2,1)}), bf16[1024,1536]{0,1:T(8,128)(2,1)}) %all-gather.5.cloned.1.call-update) | async-done | bytes 3145744 | tf_op jit(solution)/shard_map/all_gather | solution.py:71
  282.3 4.5 fusion.15
  286.8 67.9 %all-gather.9.cloned.1.call-done = bf16[1536,1024]{1,0:T(8,128)(2,1)} async-done(((bf16[48,1024]{1,0:T(8,128)(2,1)}), bf16[1536,1024]{1,0:T(8,128)(2,1)}) %all-gather.9.cloned.1.call-update) | async-done | bytes 3145744 | tf_op jit(solution)/shard_map/all_gather | solution.py:73
  354.7 3.0 fusion.8
  357.7 0.2 copy-done.5
  358.0 1.2 fusion.7
  359.2 0.6 copy-done.1
  359.9 1.6 multiply_reduce_fusion
  361.4 1.7 bitcast_reduce_fusion
  363.2 0.3 reduce-scatter.5.cloned.1.call-start
  363.4 68.8 %all-gather.11.cloned.1.call-done = bf16[1024,1024]{1,0:T(8,128)(2,1)} async-done(((bf16[32,1024]{1,0:T(8,128)(2,1)}), bf16[1024,1024]{1,0:T(8,128)(2,1)}) %all-gather.11.cloned.1.call-update) | async-done | bytes 2097168 | tf_op jit(solution)/shard_map/all_gather | solution.py:80
  432.2 3.1 fusion.3
  435.3 0.0 reduce-scatter.5.cloned.1.call-update
  435.4 4.8 fusion.1
  440.1 1.4 convolution_convert_fusion.1
  441.5 77.4 %reduce-scatter.5.cloned.1.call-done = bf16[128,64]{0,1:T(8,128)(2,1)} async-done(((bf16[128,1024]{0,1:T(8,128)(2,1)}), bf16[128,64]{0,1:T(8,128)(2,1)}) %reduce-scatter.5.cloned.1.call-update) | async-done | bytes 16400 | tf_op jit(solution)/shard_map/reduce_scatter | solution.py:83
  518.9 1.3 convert_element_type.55
  (20 shorter events, 0.1 us)
Async XLA Ops:
  7.2 1.0 copy-start
  7.2 124.6 %reduce-scatter.3.cloned.1.call-start = ((), (), s32[]{:S(2)}) async-start(), calls=%async_computation.3 | async-start | bytes 2162688 | tf_op jit(solution)/shard_map/reduce_scatter | solution.py:60
  11.1 2.2 copy-start.7
  11.1 198.7 %all-gather.7.cloned.1.call-start = ((), (), s32[]{:S(2)}) async-start(), calls=%async_computation.5 | async-start | bytes 3244032 | tf_op jit(solution)/shard_map/all_gather | solution.py:72
  11.8 270.5 %all-gather.5.cloned.1.call-start = ((), (), s32[]{:S(2)}) async-start(), calls=%async_computation.4 | async-start | bytes 3244032 | tf_op jit(solution)/shard_map/all_gather | solution.py:71
  12.6 342.1 %all-gather.9.cloned.1.call-start = ((), (), s32[]{:S(2)}) async-start(), calls=%async_computation.6 | async-start | bytes 3244032 | tf_op jit(solution)/shard_map/all_gather | solution.py:73
  13.1 3.0 copy-start.8
  13.2 419.1 %all-gather.11.cloned.1.call-start = ((), (), s32[]{:S(2)}) async-start(), calls=%async_computation.7 | async-start | bytes 2162688 | tf_op jit(solution)/shard_map/all_gather | solution.py:80
  213.1 141.5 %copy-start.4 = (bf16[32,8,1024]{2,1,0:T(8,128)(2,1)S(1)}, bf16[32,8,1024]{2,1,0:T(8,128)(2,1)}, u32[]{:S(2)}) copy-start(bf16[32,8,1024]{2,1,0:T(8,128)(2,1)} %param.15) | copy-start | bytes 1572868
  354.7 3.1 copy-start.2
  354.7 3.3 copy-start.5
  358.0 1.9 copy-start.1
  363.2 155.7 %reduce-scatter.5.cloned.1.call-start = ((), (), s32[]{:S(2)}) async-start(), calls=%async_computation.8 | async-start | bytes 278528 | tf_op jit(solution)/shard_map/reduce_scatter | solution.py:83
  435.3 4.8 copy-start.3
  435.4 4.8 copy-start.6
Sparse Core Ops, SparseCore 0:
  11.2 120.5 reduce-scatter.2
  134.2 75.6 all-gather.6
  212.2 70.0 all-gather.4
  284.5 70.0 all-gather.8
  363.3 68.9 all-gather.10
  436.7 82.1 reduce-scatter.4
where the time goes:
time: 528 us; the launch traced here: 527 us
  waiting for transfers between devices  400 us (76%)
  blocking collectives  46.4 us (9%)
  local copies, waits for them, and re-layouts  36.2 us (7%)
  matrix products  25.8 us (5%)
  between operations  14.3 us (3%)
    reduce_scatter x1, waiting for transfers between devices, per_device(): lax.psum_scatter(grad_term.astype(jnp.bfloat16), 'dp', scatter_dimension=...  77.4 us
    all_gather x1, waiting for transfers between devices, per_device(): lax.all_gather(up_proj, 'mp', axis=1, tiled=True)  76.8 us
    all_gather x1, waiting for transfers between devices, per_device(): lax.all_gather(gate_proj, 'mp', axis=1, tiled=True)  69.2 us
    all_gather x1, waiting for transfers between devices, per_device(): gathered_grad = lax.all_gather(context_back, 'mp', axis=0, tiled=True)  68.8 us
    all_gather x1, waiting for transfers between devices, per_device(): lax.all_gather(down_proj, 'mp', axis=0, tiled=True)  67.9 us
    all_to_all x1, blocking collectives, per_device(): lax.all_to_all(looked, 'mp', split_axis=0, concat_axis=3, tiled=True)  46.4 us
    reduce_scatter x1, waiting for transfers between devices, per_device(): lax.psum_scatter(jnp.dot(temporal, context_weight, preferred_element_type...  37.8 us
    gather x1, local copies, waits for them, and re-layouts, per_device(): looked = flat_tables[code_ids + offsets[None, :]]  21.7 us
  transfers between devices with their start and end apart: 6, of which 6 were waited for; matrix products, arithmetic and copies ran while one was open for 9% of the time, Pallas kernels for 0%

commit v1 on v0

v1 whole, which is shorter than its diff:
```python
import functools

import jax
import jax.numpy as jnp
from jax import lax
from jax.experimental import pallas as pl
from jax.experimental.pallas import tpu as pltpu
from jax.sharding import PartitionSpec as P

NX = 4
LANES = 128
BF16 = jnp.bfloat16
F32 = jnp.float32
MESH = pl.DeviceIdType.MESH


def dot_t(left, right):
    return lax.dot_general(left, right, (((1,), (1,)), ((), ())), preferred_element_type=F32)


def dot(left, right):
    return lax.dot_general(left, right, (((1,), (0,)), ((), ())), preferred_element_type=F32)


def copy_to(src, dst, send, recv, device):
    return pltpu.make_async_remote_copy(
        src_ref=src, dst_ref=dst, send_sem=send, recv_sem=recv, device_id=device, device_id_type=MESH
    )


def kernel(
    n_dp, n_mp,
    temporal, codes, ctx_weight, tables, gate_t, up_t, down, out_grad,
    out, temporal_grad, context_grad,
    wall, tx, wx, sums, rs_s, rs_r, xs, yb, rr, ctx, ctx_s, temporal_t,
    inp, nrm, nlow, inv, hid, ngrad, cback, cg_s, cg_r,
    z_s, z_r, x1_s, x1_r, x2_s, x2_r, y_s, y_r, c_s, c_r, rsum_s, rsum_r,
    a2a_s, a2a_r, gz_s, gz_r, gc_s, gc_r, dp_s, dp_r, ex_s, ex_r,
):
    nz = n_mp // 2
    nh = nz // 2
    ny = n_dp // NX
    dp, mp = lax.axis_index("dp"), lax.axis_index("mp")
    x, y = lax.rem(dp, NX), lax.div(dp, NX)
    z, c = lax.div(mp, 2), lax.rem(mp, 2)
    o = 1 - c
    par = lax.rem(y, 2)
    steps = temporal.shape[0]
    sdev = steps // n_mp
    width = ctx_weight.shape[1]
    half = width // 2
    rows = 8 * sdev
    unit = gate_t.shape[0]
    ff = wall.shape[1]

    def wrap(v, n):
        return lax.rem(v + 2 * n, n)

    def at_z(zz, cc):
        return (dp, wrap(zz, nz) * 2 + cc)

    def at_plane(yy, xx):
        return (wrap(yy, ny) * NX + wrap(xx, NX), mp)

    zp, zm = at_z(z + 1, c), at_z(z - 1, c)
    xp, xm = at_plane(y, x + 1), at_plane(y, x - 1)
    yp, ym = at_plane(y + 1, x), at_plane(y - 1, x)
    other = (dp, z * 2 + o)

    barrier = pltpu.get_barrier_semaphore()

    def greet_mp(k, carry):
        pl.semaphore_signal(barrier, inc=1, device_id=(dp, lax.rem(mp + k, n_mp)), device_id_type=MESH)
        return carry

    def greet_dp(k, carry):
        pl.semaphore_signal(barrier, inc=1, device_id=(lax.rem(dp + k, n_dp), mp), device_id_type=MESH)
        return carry

    lax.fori_loop(1, n_mp, greet_mp, 0)
    lax.fori_loop(1, n_dp, greet_dp, 0)

    def w_at(cc, zs, lane, count):
        row = pl.multiple_of((cc * nz + wrap(zs, nz)) * unit, 16)
        return wall.at[:, pl.ds(row, unit), pl.ds(pl.multiple_of(lane, LANES), count)]

    def tile_of(xx):
        return (par * NX + wrap(xx, NX)) * LANES

    mine = tile_of(x)
    row0 = pl.multiple_of((c * nz + z) * unit, 16)
    lane0 = pl.multiple_of(mine, LANES)
    for index, shard in enumerate((gate_t, up_t, down)):
        wall[index, pl.ds(row0, unit), pl.ds(lane0, LANES)] = shard[:, pl.ds(lane0, LANES)]

    pl.semaphore_wait(barrier, n_mp - 1 + n_dp - 1)

    def origin(d, i):
        return z - 1 - i if d == 0 else z + i

    def w_z(d, i, cc):
        zs = origin(d, i)
        return lambda k: copy_to(
            w_at(cc, zs, mine, LANES), w_at(cc, zs, mine, LANES), z_s.at[d * nh + k], z_r.at[d * nh + k],
            zp if d == 0 else zm,
        )

    half_lane = pl.multiple_of(c * half, LANES)
    other_lane = pl.multiple_of(o * half, LANES)
    feat = temporal.shape[1]
    own_feat = pl.multiple_of(c * feat, LANES)
    ex_t = copy_to(temporal, tx.at[:, pl.ds(own_feat, feat)], ex_s.at[0], ex_r.at[0], other)
    ex_w = copy_to(
        ctx_weight.at[:, pl.ds(other_lane, half)], wx.at[pl.ds(own_feat, feat), :], ex_s.at[1], ex_r.at[1], other
    )
    ex_t.start()
    ex_w.start()
    w_z(0, -1, c)(0).start()
    tx[:, pl.ds(own_feat, feat)] = temporal[...]
    wx[pl.ds(own_feat, feat), :] = ctx_weight[:, pl.ds(half_lane, half)]

    groups = n_mp // 4

    def lookup(level, carry):
        code = codes[pl.ds(level, 1), :]
        low = jnp.bitwise_and(code, 255)
        high = lax.shift_right_logical(code, 8)
        table = tables[level]
        parts = table.shape[1] // 256
        stacked = jnp.concatenate([table[:, a * 256 : (a + 1) * 256] for a in range(parts)], axis=0)
        lane = pl.multiple_of(level * LANES, LANES)
        per = min(256, steps)
        for q in range(steps // per):
            piece = slice(q * per, (q + 1) * per)
            hot = (lax.broadcasted_iota(jnp.int32, (256, per), 0) == low[:, piece]).astype(F32).astype(BF16)
            picked = dot(stacked, hot)
            fsize = table.shape[0]
            total = jnp.zeros((fsize, per), F32)
            for a in range(parts):
                total = total + jnp.where(high[:, piece] == a, picked[a * fsize : (a + 1) * fsize, :], 0.0)
            total = total.astype(BF16)
            for e in range(per // LANES):
                g = q * (per // LANES) + e
                xs[g * fsize : (g + 1) * fsize, pl.ds(lane, LANES)] = total[:, e * LANES : (e + 1) * LANES]
        return carry

    levels = codes.shape[0]
    lax.fori_loop(0, levels, lookup, 0)
    for level in range(levels, 8):
        xs[:, level * LANES : (level + 1) * LANES] = jnp.zeros((xs.shape[0], LANES), BF16)
    r_id = lax.broadcasted_iota(jnp.int32, (512, 512), 0)
    c_id = lax.broadcasted_iota(jnp.int32, (512, 512), 1)
    moved = (
        jnp.bitwise_and(lax.shift_right_logical(r_id, 5), 3) * 128
        + lax.shift_right_logical(r_id, 7) * 32
        + jnp.bitwise_and(r_id, 31)
    )
    perm = (moved == c_id).astype(F32).astype(BF16)
    fsize = tables.shape[1]
    for h in range(2):
        spread = dot(xs[:, h * 512 : (h + 1) * 512], perm).astype(BF16)
        for g in range(groups):
            for e in range(4):
                yb[4 * g + e, :, h * LANES : (h + 1) * LANES] = spread[
                    g * fsize : (g + 1) * fsize, e * LANES : (e + 1) * LANES
                ]

    def a2a(target):
        return copy_to(yb.at[target], rr.at[mp], a2a_s.at[target], a2a_r.at[mp], (dp, target))

    a2a(z * 2 + o).start()
    rr[mp] = yb[mp]

    ex_t.wait_recv()
    ex_w.wait_recv()
    chunk = min(256, steps)

    def term(k, carry):
        at = pl.ds(pl.multiple_of(k * chunk, chunk), chunk)
        sums[at, :] = dot(tx[at, :], wx[...])
        return carry

    lax.fori_loop(0, steps // chunk, term, 0)

    chip = 2 * sdev

    def term_of(zd):
        return sums[pl.ds(pl.multiple_of(wrap(zd, nz) * chip, 16), chip), :]

    def ring_sum(d, i):
        k = d * nh + i
        return copy_to(rs_s.at[k], rs_r.at[k], rsum_s.at[k], rsum_r.at[k], zp if d == 0 else zm)

    def dest(d, i):
        return z + (nh - 1) - i if d == 0 else z - nh + i

    for d in (0, 1):
        rs_s[d * nh] = term_of(dest(d, 0)).astype(BF16)
        ring_sum(d, 0).start()

    def w_x1(d, side, i):
        k = (d * 2 + side) * nh + i
        block = w_at(c, origin(d, i), mine, LANES)
        return copy_to(block, block, x1_s.at[k], x1_r.at[k], xp if side == 0 else xm)

    def w_x2(d, i):
        block = w_at(c, origin(d, i), tile_of(x - 1 if d == 0 else x + 1), LANES)
        return copy_to(block, block, x2_s.at[d * nh + i], x2_r.at[d * nh + i], xp if d == 0 else xm)

    def w_y(d, i):
        block = w_at(c, origin(d, i), par * NX * LANES, NX * LANES)
        return copy_to(block, block, y_s.at[d * nh + i], y_r.at[d * nh + i], yp if d == 0 else ym)

    def w_c(d, i, cc):
        block = w_at(cc, origin(d, i), 0, width)
        return copy_to(block, block, c_s.at[d * nh + i], c_r.at[d * nh + i], other)

    def early(i, carry):
        for d in (0, 1):
            last = nh - 2 if d == 0 else nh - 1

            @pl.when(i < last)
            def _():
                ring_sum(d, i).wait_recv()
                rs_s[d * nh + i + 1] = (
                    term_of(dest(d, i + 1)) + rs_r[d * nh + i].astype(F32)
                ).astype(BF16)
                ring_sum(d, i + 1).start()

        @pl.when(i == nh)
        def _():
            ring_sum(0, nh - 2).wait_recv()
            ring_sum(1, nh - 1).wait_recv()
            total = term_of(z) + rs_r[nh - 2].astype(F32) + rs_r[2 * nh - 1].astype(F32)
            first = c == 0
            ctx[:, pl.ds(half_lane, half)] = jnp.where(first, total[:sdev], total[sdev:])
            ctx_s[...] = jnp.where(first, total[sdev:], total[:sdev])
            copy_to(ctx_s, ctx.at[:, pl.ds(half_lane, half)], ex_s.at[2], ex_r.at[2], other).start()

        @pl.when(i < nh)
        def _():
            w_z(0, i, c)(i).wait_recv()

            @pl.when(i > 0)
            def _():
                w_z(1, i, c)(i).wait_recv()

            @pl.when(i < nh - 1)
            def _():
                w_z(0, i, c)(i + 1).start()
                w_z(1, i, c)(i + 1).start()

            for d in (0, 1):
                for side in (0, 1):
                    w_x1(d, side, i).start()

            for cc in (0, 1):
                a2a(wrap(z + nh - i, nz) * 2 + cc).start()

            @pl.when(i > 0)
            def _():
                for cc in (0, 1):
                    a2a(wrap(z - nh + i, nz) * 2 + cc).start()

        @pl.when(jnp.logical_and(i >= 1, i < nh + 1))
        def _():
            for d in (0, 1):
                for side in (0, 1):
                    w_x1(d, side, i - 1).wait_recv()
            for d in (0, 1):
                w_x2(d, i - 1).start()

        @pl.when(jnp.logical_and(i >= 2, i < nh + 2))
        def _():
            for d in (0, 1):
                w_x2(d, i - 2).wait_recv()
                w_y(d, i - 2).start()

        @pl.when(i >= 3)
        def _():
            for d in (0, 1):
                w_y(d, i - 3).wait_recv()
                w_c(d, i - 3, c).start()

        return carry

    lax.fori_loop(0, nh + 3, early, 0)

    temporal_t[...] = temporal[...].astype(F32).T.astype(BF16)

    def await_a2a(k, carry):
        copy_to(yb.at[k], rr.at[k], a2a_s.at[k], a2a_r.at[k], other).wait_recv()
        return carry

    lax.fori_loop(0, mp, await_a2a, 0)
    lax.fori_loop(mp + 1, n_mp, await_a2a, 0)
    copy_to(ctx_s, ctx.at[:, pl.ds(other_lane, half)], ex_s.at[2], ex_r.at[2], other).wait_recv()

    p_row = lax.broadcasted_iota(jnp.int32, (rows, 256), 0)
    p_col = lax.broadcasted_iota(jnp.int32, (rows, 256), 1)
    p_lane = (jnp.bitwise_and(p_row, 7) - 1) * 32 + lax.shift_right_logical(p_row, 3)
    place = (p_lane == p_col).astype(F32).astype(BF16)
    inp[...] = dot_t(place, rr[...].reshape(n_mp * fsize, 256))

    part = 64

    def normalise(k, carry):
        at = pl.ds(pl.multiple_of(k * part, part), part)
        base = ctx[pl.ds(pl.multiple_of(k * (part // 8), 8), part // 8), :]
        value = inp[at, :] + jnp.broadcast_to(base[:, None, :], (part // 8, 8, width)).reshape(part, width)
        scale = lax.rsqrt(jnp.mean(value * value, axis=-1, keepdims=True) + 1e-06)
        normed = value * scale
        inp[at, :] = value
        nrm[at, :] = normed
        nlow[at, :] = normed.astype(BF16)
        inv[at, :] = jnp.broadcast_to(scale, (part, LANES))
        ngrad[at, :] = jnp.zeros((part, width), F32)
        return carry

    lax.fori_loop(0, rows // part, normalise, 0)

    def await_w(k, carry):
        for d in (0, 1):
            w_c(d, k, o).wait_recv()
        return carry

    lax.fori_loop(0, nh, await_w, 0)

    fchunk = 256 if ff % 256 == 0 else 128

    def depth(k, carry):
        at = pl.ds(pl.multiple_of(k * fchunk, fchunk), fchunk)
        gate = dot_t(nlow[...], wall[0, at, :])
        upper = dot_t(nlow[...], wall[1, at, :])
        hgrad = dot_t(out_grad[...], wall[2, at, :])
        sig = jax.nn.sigmoid(gate)
        act = gate * sig
        hid[:, at] = (act * upper).astype(BF16)
        ggrad = (hgrad * upper * sig * (1.0 + gate * (1.0 - sig))).astype(BF16)
        ugrad = (hgrad * act).astype(BF16)
        ngrad[...] += dot(ggrad, wall[0, at, :]) + dot(ugrad, wall[1, at, :])
        return carry

    lax.fori_loop(0, ff // fchunk, depth, 0)

    def back(k, carry):
        at = pl.ds(pl.multiple_of(k * 128, 128), 128)
        grad, normed = ngrad[at, :], nrm[at, :]
        inner = jnp.mean(grad * normed, axis=-1, keepdims=True)
        total = out_grad[at, :].astype(F32) + inv[at, :1] * (grad - normed * inner)
        summed = jnp.sum(total.reshape(16, 8, width), axis=1)
        cback[pl.ds(pl.multiple_of(mp * sdev + k * 16, 16), 16), :] = summed.astype(BF16)
        return carry

    lax.fori_loop(0, rows // 128, back, 0)

    def g_at(zs, cc):
        return cback.at[pl.ds(pl.multiple_of((wrap(zs, nz) * 2 + cc) * sdev, 16), sdev), :]

    def g_z(d, i, k):
        block = g_at(origin(d, i), c)
        return copy_to(block, block, gz_s.at[d * nh + k], gz_r.at[d * nh + k], zp if d == 0 else zm)

    def g_c(d, i, cc):
        block = g_at(origin(d, i), cc)
        return copy_to(block, block, gc_s.at[d * nh + i], gc_r.at[d * nh + i], other)

    g_z(0, -1, 0).start()
    inv_n = 1.0 / steps
    n_chunks = width // 256

    def late(i, carry):
        @pl.when(i > 0)
        def _():
            g_z(0, i - 1, i - 1).wait_recv()

            @pl.when(i < nh)
            def _():
                g_z(0, i - 1, i).start()

            g_c(0, i - 1, c).start()

        @pl.when(i < nh)
        def _():
            @pl.when(i > 0)
            def _():
                g_z(1, i, i).wait_recv()

            @pl.when(i < nh - 1)
            def _():
                g_z(1, i, i + 1).start()

            g_c(1, i, c).start()

        @pl.when(i < n_chunks)
        def _():
            at = pl.ds(pl.multiple_of(i * 256, 256), 256)
            out[:, at] = (inp[:, at] + dot(hid[...], wall[2, :, at])).astype(BF16)

        return carry

    lax.fori_loop(0, nh + 1, late, 0)

    def await_g(k, carry):
        for d in (0, 1):
            g_c(d, k, o).wait_recv()
        return carry

    lax.fori_loop(0, nh, await_g, 0)

    cols = width // n_dp
    cg_s[...] = (dot(temporal_t[...], cback[...]) * inv_n).T.astype(BF16)

    def cg(target):
        block = cg_s.at[pl.ds(pl.multiple_of(target * cols, 16), cols), :]
        return copy_to(block, cg_r.at[dp], dp_s.at[target], dp_r.at[dp], (target, mp))

    def send_cg(k, carry):
        cg(lax.rem(dp + k, n_dp)).start()
        return carry

    lax.fori_loop(1, n_dp, send_cg, 0)
    cg_r[dp] = cg_s[pl.ds(pl.multiple_of(dp * cols, 16), cols), :]

    def tgrad(k, carry):
        at = pl.ds(pl.multiple_of(k * chunk, chunk), chunk)
        temporal_grad[at, :] = dot_t(cback[at, :], ctx_weight[...]).astype(BF16)
        return carry

    lax.fori_loop(0, steps // chunk, tgrad, 0)

    ex_t.wait_send()
    ex_w.wait_send()
    copy_to(ctx_s, ctx.at[:, pl.ds(half_lane, half)], ex_s.at[2], ex_r.at[2], other).wait_send()

    def sent(i, carry):
        w_z(0, i, c)(i).wait_send()
        g_z(0, i, i).wait_send()
        ring_sum(1, i).wait_send()

        @pl.when(i > 0)
        def _():
            w_z(1, i, c)(i).wait_send()
            g_z(1, i, i).wait_send()

        @pl.when(i < nh - 1)
        def _():
            ring_sum(0, i).wait_send()

        for d in (0, 1):
            for side in (0, 1):
                w_x1(d, side, i).wait_send()
            w_x2(d, i).wait_send()
            w_y(d, i).wait_send()
            w_c(d, i, c).wait_send()
            g_c(d, i, c).wait_send()
        return carry

    lax.fori_loop(0, nh, sent, 0)

    def sent_a2a(k, carry):
        a2a(lax.rem(mp + k, n_mp)).wait_send()
        return carry

    lax.fori_loop(1, n_mp, sent_a2a, 0)

    def await_cg(k, carry):
        source = lax.rem(dp + k, n_dp)
        copy_to(cg_r.at[source], cg_r.at[source], dp_s.at[source], dp_r.at[source], other).wait_recv()
        cg(source).wait_send()
        return carry

    lax.fori_loop(1, n_dp, await_cg, 0)
    total = cg_r[0].astype(F32)
    for k in range(1, n_dp):
        total = total + cg_r[k].astype(F32)
    context_grad[...] = total


def per_device(
    n_dp, n_mp, temporal, code_ids, context_weight, code_tables, gate_proj, up_proj, down_proj, out_grad
):
    steps, feat = temporal.shape
    sdev, levels, width = out_grad.shape
    rows = sdev * levels
    unit = down_proj.shape[0]
    ff = unit * n_mp
    nh = n_mp // 4
    cols = width // n_dp
    half = width // 2
    fsize = code_tables.shape[2]
    vmem = pl.BlockSpec(memory_space=pltpu.VMEM)
    dma = lambda n: pltpu.SemaphoreType.DMA((n,))
    scratch = [
        pltpu.VMEM((3, ff, width), BF16),
        pltpu.VMEM((steps, 2 * feat), BF16),
        pltpu.VMEM((2 * feat, half), BF16),
        pltpu.VMEM((steps, half), F32),
        pltpu.VMEM((2 * nh, 2 * sdev, half), BF16),
        pltpu.VMEM((2 * nh, 2 * sdev, half), BF16),
        pltpu.VMEM((fsize * n_mp // 4, 8 * LANES), BF16),
        pltpu.VMEM((n_mp, fsize, 256), BF16),
        pltpu.VMEM((n_mp, fsize, 256), BF16),
        pltpu.VMEM((sdev, width), F32),
        pltpu.VMEM((sdev, half), F32),
        pltpu.VMEM((feat, steps), BF16),
        pltpu.VMEM((rows, width), F32),
        pltpu.VMEM((rows, width), F32),
        pltpu.VMEM((rows, width), BF16),
        pltpu.VMEM((rows, LANES), F32),
        pltpu.VMEM((rows, ff), BF16),
        pltpu.VMEM((rows, width), F32),
        pltpu.VMEM((steps, width), BF16),
        pltpu.VMEM((width, feat), BF16),
        pltpu.VMEM((n_dp, cols, feat), BF16),
    ]
    sems = [2 * nh, 4 * nh, 2 * nh, 2 * nh, 2 * nh, 2 * nh, n_mp, 2 * nh, 2 * nh, n_dp, 3]
    for n in sems:
        scratch += [dma(n), dma(n)]
    out, tgrad, cgrad = pl.pallas_call(
        functools.partial(kernel, n_dp, n_mp),
        out_shape=(
            jax.ShapeDtypeStruct((rows, width), BF16),
            jax.ShapeDtypeStruct((steps, feat), BF16),
            jax.ShapeDtypeStruct((cols, feat), F32),
        ),
        in_specs=[vmem] * 8,
        out_specs=(vmem, vmem, vmem),
        scratch_shapes=scratch,
        compiler_params=pltpu.CompilerParams(
            collective_id=0, has_side_effects=True, vmem_limit_bytes=58 * 1024 * 1024
        ),
        cost_estimate=pl.CostEstimate(
            flops=2 * rows * width * ff * 6 + 6 * steps * feat * width, bytes_accessed=4 * 2**20, transcendentals=0
        ),
        name="depth_block",
    )(
        temporal,
        code_ids.T,
        context_weight,
        code_tables.transpose(0, 2, 1),
        gate_proj.T,
        up_proj.T,
        down_proj,
        out_grad.reshape(rows, width),
    )
    return out.reshape(sdev, levels, width), tgrad, cgrad.T


def solution(mesh):
    in_specs = (
        P("dp", "mp"),
        P("dp", None),
        P("mp", None),
        P(None, None, "mp"),
        P(None, "mp"),
        P(None, "mp"),
        P("mp", None),
        P(("dp", "mp"), None, None),
    )
    out_specs = (P(("dp", "mp"), None, None), P("dp", "mp"), P("mp", "dp"))
    return jax.shard_map(
        functools.partial(per_device, mesh.shape["dp"], mesh.shape["mp"]),
        mesh=mesh,
        in_specs=in_specs,
        out_specs=out_specs,
        check_vma=False,
    )
```

time: 528 us -> 133 us (0.25)
  waiting for transfers between devices: 400 us -> 0 us
  Pallas kernels: 0 us -> 129 us
  blocking collectives: 46.4 us -> 0 us
  local copies, waits for them, and re-layouts: 36.2 us -> 3.29 us
  matrix products: 25.8 us -> 0 us
  between operations: 14.3 us -> 0.65 us
    all_gather x4 -> x0, waiting for transfers between devices: 283 us -> none  [the longest x1 76.8 us: per_device(): lax.all_gather(up_proj, 'mp', axis=1, tiled=True)]
    pallas_call x0 -> x1, Pallas kernels: none -> 129 us  [per_device(): pl.pallas_call(functools.partial(kernel, n_dp, n_mp), out_shape=(jax.Shap...]
    reduce_scatter x2 -> x0, waiting for transfers between devices: 115 us -> none  [the longest x1 77.4 us: per_device(): lax.psum_scatter(grad_term.astype(jnp.bfloat16), 'dp', scatter_dimension=...]
    all_to_all x1 -> x0, blocking collectives: 46.4 us -> none  [per_device(): lax.all_to_all(looked, 'mp', split_axis=0, concat_axis=3, tiled=True)]
    dot_general x9 -> x0, matrix products: 25.8 us -> none  [the longest x4 7.29 us: contract_last(): lax.dot_general(left, right, (((1,), (1,)), ((), ())), preferred_element_...]
    gather x1 -> x0, local copies, waits for them, and re-layouts: 21.7 us -> none  [per_device(): looked = flat_tables[code_ids + offsets[None, :]]]
    reshape x3 -> x0, local copies, waits for them, and re-layouts: 5.61 us -> none  [the longest x2 3.66 us: per_device(): looked.reshape(groups, steps_dev, inputs_levels, code_tables.shape[2])]
  transfers between devices with their start and end apart: 6 -> 0, of which waited for: 6 -> 0; matrix products, arithmetic and copies ran while one was open for 9% -> 0% of each run, Pallas kernels for 0% -> 0%
where the time goes in v1:
time: 133 us
  Pallas kernels  129 us (97%)
  local copies, waits for them, and re-layouts  3.29 us (2%)
    pallas_call x1, Pallas kernels, per_device(): pl.pallas_call(functools.partial(kernel, n_dp, n_mp), out_shape=(jax.Shap...  129 us
    unnamed x7, local copies, waits for them, and re-layouts  3.29 us

profile of v1, /device:TPU:1, one launch (start us, length us, event | category | flops | bytes accessed | tf_op | source)
XLA Modules:
  0.0 132.8 jit_solution(3707633159101605703)
XLA Ops:
  0.6 128.8 %depth_block.1 = (bf16[256,1024]{1,0:T(8,128)(2,1)}, bf16[1024,128]{1,0:T(8,128)(2,1)}, f32[64,128]{1,0:T(8,128)}) custom-call(bf16[1024,128]{1,0:T(8,128)(2,1)} %temporal.1, s32[7,1024]{1,0:T(8,128)} %bitcast.13, bf16[128,1024]{1,0:T(8,128)(2,1)} %ctx_weight.1, bf16[7,32,2048]{2,1,0:T(8,128)(2,1)} %bitcast.9, bf16[48,1024]{1,0:T(8,128)(2,1)} %bitcast.11, ...), custom_call_target="tpu_custom_call" | custom-call | flops 5637144576 | bytes 4194304 | tf_op jit(solution)/shard_map/depth_block/pallas_call | solution.py:520
  129.5 0.0 copy-start
  129.5 1.9 %copy.14 = bf16[32,8,1024]{2,1,0:T(8,128)(2,1)} copy(bf16[32,8,1024]{2,1,0:T(8,128)(2,1)} %bitcast.7) | data formatting | bytes 1048576
  131.4 0.0 copy-done
  131.4 0.0 copy-start.1
  131.4 0.7 copy.15
  132.1 0.1 copy-done.1
  132.2 0.6 copy.16
Async XLA Ops:
  129.5 1.9 %copy-start = (bf16[1024,128]{1,0:T(8,128)(2,1)S(1)}, bf16[1024,128]{1,0:T(8,128)(2,1)}, u32[]{:S(2)}) copy-start(bf16[1024,128]{1,0:T(8,128)(2,1)} %get-tuple-element.13) | copy-start | bytes 786436
  131.4 0.8 copy-start.1

commit v2 on v1

--- a/solution.py
+++ b/solution.py
@@ -33,7 +33,7 @@
     temporal, codes, ctx_weight, tables, gate_t, up_t, down, out_grad,
     out, temporal_grad, context_grad,
     wall, tx, wx, sums, rs_s, rs_r, xs, yb, rr, ctx, ctx_s, temporal_t,
-    inp, nrm, nlow, inv, hid, ngrad, cback, cg_s, cg_r,
+    inp, nrm, nlow, inv, hid, hback, ngrad, cback, cg_s, cg_r,
     z_s, z_r, x1_s, x1_r, x2_s, x2_r, y_s, y_r, c_s, c_r, rsum_s, rsum_r,
     a2a_s, a2a_r, gz_s, gz_r, gc_s, gc_r, dp_s, dp_r, ex_s, ex_r,
 ):
@@ -134,7 +134,6 @@
             piece = slice(q * per, (q + 1) * per)
             hot = (lax.broadcasted_iota(jnp.int32, (256, per), 0) == low[:, piece]).astype(F32).astype(BF16)
             picked = dot(stacked, hot)
-            fsize = table.shape[0]
             total = jnp.zeros((fsize, per), F32)
             for a in range(parts):
                 total = total + jnp.where(high[:, piece] == a, picked[a * fsize : (a + 1) * fsize, :], 0.0)
@@ -145,32 +144,32 @@
         return carry
 
     levels = codes.shape[0]
-    lax.fori_loop(0, levels, lookup, 0)
-    for level in range(levels, 8):
-        xs[:, level * LANES : (level + 1) * LANES] = jnp.zeros((xs.shape[0], LANES), BF16)
-    r_id = lax.broadcasted_iota(jnp.int32, (512, 512), 0)
-    c_id = lax.broadcasted_iota(jnp.int32, (512, 512), 1)
-    moved = (
-        jnp.bitwise_and(lax.shift_right_logical(r_id, 5), 3) * 128
-        + lax.shift_right_logical(r_id, 7) * 32
-        + jnp.bitwise_and(r_id, 31)
-    )
-    perm = (moved == c_id).astype(F32).astype(BF16)
     fsize = tables.shape[1]
-    for h in range(2):
-        spread = dot(xs[:, h * 512 : (h + 1) * 512], perm).astype(BF16)
-        for g in range(groups):
-            for e in range(4):
-                yb[4 * g + e, :, h * LANES : (h + 1) * LANES] = spread[
-                    g * fsize : (g + 1) * fsize, e * LANES : (e + 1) * LANES
-                ]
+
+    def arrange():
+        for level in range(levels, 8):
+            xs[:, level * LANES : (level + 1) * LANES] = jnp.zeros((xs.shape[0], LANES), BF16)
+        r_id = lax.broadcasted_iota(jnp.int32, (512, 512), 0)
+        c_id = lax.broadcasted_iota(jnp.int32, (512, 512), 1)
+        moved = (
+            jnp.bitwise_and(lax.shift_right_logical(r_id, 5), 3) * 128
+            + lax.shift_right_logical(r_id, 7) * 32
+            + jnp.bitwise_and(r_id, 31)
+        )
+        perm = (moved == c_id).astype(F32).astype(BF16)
+        for h in range(2):
+            spread = dot(xs[:, h * 512 : (h + 1) * 512], perm).astype(BF16)
+            for g in range(groups):
+                for e in range(4):
+                    yb[4 * g + e, :, h * LANES : (h + 1) * LANES] = spread[
+                        g * fsize : (g + 1) * fsize, e * LANES : (e + 1) * LANES
+                    ]
+        rr[mp] = yb[mp]
 
     def a2a(target):
         return copy_to(yb.at[target], rr.at[mp], a2a_s.at[target], a2a_r.at[mp], (dp, target))
 
-    a2a(z * 2 + o).start()
-    rr[mp] = yb[mp]
-
+    temporal_t[...] = temporal[...].astype(F32).T.astype(BF16)
     ex_t.wait_recv()
     ex_w.wait_recv()
     chunk = min(256, steps)
@@ -214,6 +213,8 @@
     def w_c(d, i, cc):
         block = w_at(cc, origin(d, i), 0, width)
         return copy_to(block, block, c_s.at[d * nh + i], c_r.at[d * nh + i], other)
+
+    first_send = nh // 2
 
     def early(i, carry):
         for d in (0, 1):
@@ -254,14 +255,6 @@
                 for side in (0, 1):
                     w_x1(d, side, i).start()
 
-            for cc in (0, 1):
-                a2a(wrap(z + nh - i, nz) * 2 + cc).start()
-
-            @pl.when(i > 0)
-            def _():
-                for cc in (0, 1):
-                    a2a(wrap(z - nh + i, nz) * 2 + cc).start()
-
         @pl.when(jnp.logical_and(i >= 1, i < nh + 1))
         def _():
             for d in (0, 1):
@@ -282,11 +275,49 @@
                 w_y(d, i - 3).wait_recv()
                 w_c(d, i - 3, c).start()
 
+        @pl.when(i < first_send)
+        def _():
+            lax.fori_loop(2 * i, jnp.minimum(2 * i + 2, levels), lookup, 0)
+
+        @pl.when(i == first_send - 1)
+        def _():
+            arrange()
+
+        @pl.when(i == first_send)
+        def _():
+            a2a(z * 2 + o).start()
+
+        @pl.when(jnp.logical_and(i >= first_send, i < nh))
+        def _():
+            for e in (0, 1):
+                apart = nh - 2 * (i - first_send) - e
+                for cc in (0, 1):
+                    a2a(wrap(z + apart, nz) * 2 + cc).start()
+
+                @pl.when(apart < nh)
+                def _():
+                    for cc in (0, 1):
+                        a2a(wrap(z - apart, nz) * 2 + cc).start()
+
         return carry
 
     lax.fori_loop(0, nh + 3, early, 0)
 
-    temporal_t[...] = temporal[...].astype(F32).T.astype(BF16)
+    def await_w(k, carry):
+        for d in (0, 1):
+            w_c(d, k, o).wait_recv()
+        return carry
+
+    lax.fori_loop(0, nh, await_w, 0)
+
+    fchunk = 256 if ff % 256 == 0 else 128
+
+    def hidden_back(k, carry):
+        at = pl.ds(pl.multiple_of(k * fchunk, fchunk), fchunk)
+        hback[:, at] = dot_t(out_grad[...], wall[2, at, :])
+        return carry
+
+    lax.fori_loop(0, ff // fchunk, hidden_back, 0)
 
     def await_a2a(k, carry):
         copy_to(yb.at[k], rr.at[k], a2a_s.at[k], a2a_r.at[k], other).wait_recv()
@@ -319,20 +350,11 @@
 
     lax.fori_loop(0, rows // part, normalise, 0)
 
-    def await_w(k, carry):
-        for d in (0, 1):
-            w_c(d, k, o).wait_recv()
-        return carry
-
-    lax.fori_loop(0, nh, await_w, 0)
-
-    fchunk = 256 if ff % 256 == 0 else 128
-
     def depth(k, carry):
         at = pl.ds(pl.multiple_of(k * fchunk, fchunk), fchunk)
         gate = dot_t(nlow[...], wall[0, at, :])
         upper = dot_t(nlow[...], wall[1, at, :])
-        hgrad = dot_t(out_grad[...], wall[2, at, :])
+        hgrad = hback[:, at]
         sig = jax.nn.sigmoid(gate)
         act = gate * sig
         hid[:, at] = (act * upper).astype(BF16)
@@ -343,53 +365,61 @@
 
     lax.fori_loop(0, ff // fchunk, depth, 0)
 
+    part_g = sdev // 2
+
+    def g_rows(zs, cc, first, count):
+        return cback.at[pl.ds(pl.multiple_of((wrap(zs, nz) * 2 + cc) * sdev + first, 16), count), :]
+
+    def g_z(d, i, k, h):
+        block = g_rows(origin(d, i), c, h * part_g, part_g)
+        at = (d * nh + k) * 2 + h
+        return copy_to(block, block, gz_s.at[at], gz_r.at[at], zp if d == 0 else zm)
+
+    def g_c(d, i, cc):
+        block = g_rows(origin(d, i), cc, 0, sdev)
+        return copy_to(block, block, gc_s.at[d * nh + i], gc_r.at[d * nh + i], other)
+
     def back(k, carry):
-        at = pl.ds(pl.multiple_of(k * 128, 128), 128)
+        at = pl.ds(pl.multiple_of(k * (rows // 2), rows // 2), rows // 2)
         grad, normed = ngrad[at, :], nrm[at, :]
         inner = jnp.mean(grad * normed, axis=-1, keepdims=True)
         total = out_grad[at, :].astype(F32) + inv[at, :1] * (grad - normed * inner)
-        summed = jnp.sum(total.reshape(16, 8, width), axis=1)
-        cback[pl.ds(pl.multiple_of(mp * sdev + k * 16, 16), 16), :] = summed.astype(BF16)
-        return carry
-
-    lax.fori_loop(0, rows // 128, back, 0)
-
-    def g_at(zs, cc):
-        return cback.at[pl.ds(pl.multiple_of((wrap(zs, nz) * 2 + cc) * sdev, 16), sdev), :]
-
-    def g_z(d, i, k):
-        block = g_at(origin(d, i), c)
-        return copy_to(block, block, gz_s.at[d * nh + k], gz_r.at[d * nh + k], zp if d == 0 else zm)
-
-    def g_c(d, i, cc):
-        block = g_at(origin(d, i), cc)
-        return copy_to(block, block, gc_s.at[d * nh + i], gc_r.at[d * nh + i], other)
-
-    g_z(0, -1, 0).start()
+        summed = jnp.sum(total.reshape(part_g, 8, width), axis=1)
+        cback[pl.ds(pl.multiple_of(mp * sdev + k * part_g, 16), part_g), :] = summed.astype(BF16)
+        g_z(0, -1, 0, k).start()
+        g_z(1, 0, 1, k).start()
+        return carry
+
+    lax.fori_loop(0, 2, back, 0)
+
     inv_n = 1.0 / steps
     n_chunks = width // 256
 
     def late(i, carry):
-        @pl.when(i > 0)
-        def _():
-            g_z(0, i - 1, i - 1).wait_recv()
-
-            @pl.when(i < nh)
-            def _():
-                g_z(0, i - 1, i).start()
-
-            g_c(0, i - 1, c).start()
-
-        @pl.when(i < nh)
-        def _():
+        for h in (0, 1):
+
             @pl.when(i > 0)
             def _():
-                g_z(1, i, i).wait_recv()
-
-            @pl.when(i < nh - 1)
+                g_z(0, i - 1, i - 1, h).wait_recv()
+
+                @pl.when(i < nh)
+                def _():
+                    g_z(0, i - 1, i, h).start()
+
+            @pl.when(jnp.logical_and(i > 0, i < nh))
             def _():
-                g_z(1, i, i + 1).start()
-
+                g_z(1, i, i, h).wait_recv()
+
+                @pl.when(i < nh - 1)
+                def _():
+                    g_z(1, i, i + 1, h).start()
+
+        @pl.when(i > 0)
+        def _():
+            g_c(0, i - 1, c).start()
+
+        @pl.when(i < nh)
+        def _():
             g_c(1, i, c).start()
 
         @pl.when(i < n_chunks)
@@ -435,13 +465,15 @@
 
     def sent(i, carry):
         w_z(0, i, c)(i).wait_send()
-        g_z(0, i, i).wait_send()
+        for h in (0, 1):
+            g_z(0, i, i, h).wait_send()
         ring_sum(1, i).wait_send()
 
         @pl.when(i > 0)
         def _():
             w_z(1, i, c)(i).wait_send()
-            g_z(1, i, i).wait_send()
+            for h in (0, 1):
+                g_z(1, i, i, h).wait_send()
 
         @pl.when(i < nh - 1)
         def _():
@@ -475,6 +507,17 @@
     for k in range(1, n_dp):
         total = total + cg_r[k].astype(F32)
     context_grad[...] = total
+
+
+def hand_over(a, b, d, a_out, b_out, d_out, sems):
+    copies = [
+        pltpu.make_async_copy(src, dst, sems.at[k])
+        for k, (src, dst) in enumerate(((a, a_out), (b, b_out), (d, d_out)))
+    ]
+    for copy in copies:
+        copy.start()
+    for copy in copies:
+        copy.wait()
 
 
 def per_device(
@@ -509,12 +552,13 @@
         pltpu.VMEM((rows, width), BF16),
         pltpu.VMEM((rows, LANES), F32),
         pltpu.VMEM((rows, ff), BF16),
+        pltpu.VMEM((rows, ff), F32),
         pltpu.VMEM((rows, width), F32),
         pltpu.VMEM((steps, width), BF16),
         pltpu.VMEM((width, feat), BF16),
         pltpu.VMEM((n_dp, cols, feat), BF16),
     ]
-    sems = [2 * nh, 4 * nh, 2 * nh, 2 * nh, 2 * nh, 2 * nh, n_mp, 2 * nh, 2 * nh, n_dp, 3]
+    sems = [2 * nh, 4 * nh, 2 * nh, 2 * nh, 2 * nh, 2 * nh, n_mp, 4 * nh, 2 * nh, n_dp, 3]
     for n in sems:
         scratch += [dma(n), dma(n)]
     out, tgrad, cgrad = pl.pallas_call(
@@ -544,6 +588,15 @@
         down_proj,
         out_grad.reshape(rows, width),
     )
+    anywhere = pl.BlockSpec(memory_space=pl.ANY)
+    out, tgrad, cgrad = pl.pallas_call(
+        hand_over,
+        out_shape=tuple(jax.ShapeDtypeStruct(v.shape, v.dtype) for v in (out, tgrad, cgrad)),
+        in_specs=[anywhere] * 3,
+        out_specs=(anywhere,) * 3,
+        scratch_shapes=[dma(3)],
+        name="hand_over",
+    )(out, tgrad, cgrad)
     return out.reshape(sdev, levels, width), tgrad, cgrad.T
 
 

time: 133 us -> 153 us (1.15)
  Pallas kernels: 129 us -> 152 us
  local copies, waits for them, and re-layouts: 3.29 us -> 0 us
    pallas_call x0 -> x1, Pallas kernels: none -> 25.9 us  [per_device(): pl.pallas_call(hand_over, out_shape=tuple((jax.ShapeDtypeStruct(v.shape,...]
    unnamed x7 -> x0, local copies, waits for them, and re-layouts: 3.29 us -> none
    pallas_call x1, Pallas kernels: 129 us -> 126 us  [per_device(): pl.pallas_call(functools.partial(kernel, n_dp, n_mp), out_shape=(jax.Shap...]
where the time goes in v2:
time: 153 us
  Pallas kernels  152 us (99%)
    pallas_call x1, Pallas kernels, per_device(): pl.pallas_call(functools.partial(kernel, n_dp, n_mp), out_shape=(jax.Shap...  126 us
    pallas_call x1, Pallas kernels, per_device(): pl.pallas_call(hand_over, out_shape=tuple((jax.ShapeDtypeStruct(v.shape,...  25.9 us

profile of v2, /device:TPU:1, one launch (start us, length us, event | category | flops | bytes accessed | tf_op | source)
XLA Modules:
  0.0 152.6 jit_solution(4643273906698052551)
XLA Ops:
  0.6 126.0 %depth_block.1 = (bf16[256,1024]{1,0:T(8,128)(2,1)}, bf16[1024,128]{1,0:T(8,128)(2,1)}, f32[64,128]{1,0:T(8,128)}) custom-call(bf16[1024,128]{1,0:T(8,128)(2,1)} %temporal.1, s32[7,1024]{1,0:T(8,128)} %bitcast.12, bf16[128,1024]{1,0:T(8,128)(2,1)} %ctx_weight.1, bf16[7,32,2048]{2,1,0:T(8,128)(2,1)} %bitcast.7, bf16[48,1024]{1,0:T(8,128)(2,1)} %bitcast.10, ...), custom_call_target="tpu_custom_call" | custom-call | flops 5637144576 | bytes 4194304 | tf_op jit(solution)/shard_map/depth_block/pallas_call | solution.py:564
  126.6 25.9 %hand_over.1 = (bf16[256,1024]{1,0:T(8,128)(2,1)}, bf16[1024,128]{1,0:T(8,128)(2,1)}, f32[64,128]{1,0:T(8,128)}) custom-call(bf16[256,1024]{1,0:T(8,128)(2,1)} %get-tuple-element.9.a, bf16[1024,128]{1,0:T(8,128)(2,1)} %get-tuple-element.10.b, f32[64,128]{1,0:T(8,128)} %get-tuple-element.11.d), custom_call_target="tpu_custom_call" | custom-call | tf_op jit(solution)/shard_map/hand_over/pallas_call | solution.py:592

commit v3 on v2

--- a/solution.py
+++ b/solution.py
@@ -28,14 +28,29 @@
     )
 
 
+def swap_blocks(v):
+    lane = lax.broadcasted_iota(jnp.int32, v[0].shape, 1)
+    low = lane < 64
+    even = jnp.bitwise_and(lane, 32) == 0
+    w = [None] * 4
+    for a in (0, 1):
+        w[a] = jnp.where(low, v[a], pltpu.roll(v[a + 2], 64, 1))
+        w[a + 2] = jnp.where(low, pltpu.roll(v[a], 64, 1), v[a + 2])
+    out = [None] * 4
+    for a in (0, 2):
+        out[a] = jnp.where(even, w[a], pltpu.roll(w[a + 1], 32, 1))
+        out[a + 1] = jnp.where(even, pltpu.roll(w[a], 96, 1), w[a + 1])
+    return out
+
+
 def kernel(
     n_dp, n_mp,
     temporal, codes, ctx_weight, tables, gate_t, up_t, down, out_grad,
     out, temporal_grad, context_grad,
-    wall, tx, wx, sums, rs_s, rs_r, xs, yb, rr, ctx, ctx_s, temporal_t,
+    wall, tx, wx, sums, rs_s, rs_r, yb, rr, relay, ctx, ctx_s, temporal_t,
     inp, nrm, nlow, inv, hid, hback, ngrad, cback, cg_s, cg_r,
     z_s, z_r, x1_s, x1_r, x2_s, x2_r, y_s, y_r, c_s, c_r, rsum_s, rsum_r,
-    a2a_s, a2a_r, gz_s, gz_r, gc_s, gc_r, dp_s, dp_r, ex_s, ex_r,
+    a2a_s, a2a_r, gz_s, gz_r, gc_s, gc_r, dp_s, dp_r, ex_s, ex_r, rl_s, rl_r,
 ):
     nz = n_mp // 2
     nh = nz // 2
@@ -119,7 +134,6 @@
     tx[:, pl.ds(own_feat, feat)] = temporal[...]
     wx[pl.ds(own_feat, feat), :] = ctx_weight[:, pl.ds(half_lane, half)]
 
-    groups = n_mp // 4
 
     def lookup(level, carry):
         code = codes[pl.ds(level, 1), :]
@@ -128,7 +142,6 @@
         table = tables[level]
         parts = table.shape[1] // 256
         stacked = jnp.concatenate([table[:, a * 256 : (a + 1) * 256] for a in range(parts)], axis=0)
-        lane = pl.multiple_of(level * LANES, LANES)
         per = min(256, steps)
         for q in range(steps // per):
             piece = slice(q * per, (q + 1) * per)
@@ -137,37 +150,34 @@
             total = jnp.zeros((fsize, per), F32)
             for a in range(parts):
                 total = total + jnp.where(high[:, piece] == a, picked[a * fsize : (a + 1) * fsize, :], 0.0)
-            total = total.astype(BF16)
             for e in range(per // LANES):
                 g = q * (per // LANES) + e
-                xs[g * fsize : (g + 1) * fsize, pl.ds(lane, LANES)] = total[:, e * LANES : (e + 1) * LANES]
+                block = total[:, e * LANES : (e + 1) * LANES]
+                tiles = swap_blocks([block[8 * a : 8 * a + 8] for a in range(4)])
+                for a in range(4):
+                    yb[4 * g + a, level] = tiles[a].astype(BF16)
         return carry
 
     levels = codes.shape[0]
     fsize = tables.shape[1]
 
-    def arrange():
-        for level in range(levels, 8):
-            xs[:, level * LANES : (level + 1) * LANES] = jnp.zeros((xs.shape[0], LANES), BF16)
-        r_id = lax.broadcasted_iota(jnp.int32, (512, 512), 0)
-        c_id = lax.broadcasted_iota(jnp.int32, (512, 512), 1)
-        moved = (
-            jnp.bitwise_and(lax.shift_right_logical(r_id, 5), 3) * 128
-            + lax.shift_right_logical(r_id, 7) * 32
-            + jnp.bitwise_and(r_id, 31)
-        )
-        perm = (moved == c_id).astype(F32).astype(BF16)
-        for h in range(2):
-            spread = dot(xs[:, h * 512 : (h + 1) * 512], perm).astype(BF16)
-            for g in range(groups):
-                for e in range(4):
-                    yb[4 * g + e, :, h * LANES : (h + 1) * LANES] = spread[
-                        g * fsize : (g + 1) * fsize, e * LANES : (e + 1) * LANES
-                    ]
-        rr[mp] = yb[mp]
-
     def a2a(target):
         return copy_to(yb.at[target], rr.at[mp], a2a_s.at[target], a2a_r.at[mp], (dp, target))
+
+    quarter = nh // 2
+
+    def leg_one(cc):
+        target = wrap(z + nh, nz) * 2 + cc
+        over = z + quarter if cc == 0 else z - quarter
+        return copy_to(yb.at[target], relay.at[cc], a2a_s.at[target], rl_r.at[cc], at_z(over, c))
+
+    def leg_two(cc):
+        source, over = (z - quarter, z + quarter) if cc == 0 else (z + quarter, z - quarter)
+        origin_mp = wrap(source, nz) * 2 + c
+        return copy_to(relay.at[cc], rr.at[origin_mp], rl_s.at[cc], a2a_r.at[origin_mp], at_z(over, cc))
+
+    def await_leg(cc):
+        copy_to(relay.at[cc], relay.at[cc], rl_s.at[cc], rl_r.at[cc], other).wait_recv()
 
     temporal_t[...] = temporal[...].astype(F32).T.astype(BF16)
     ex_t.wait_recv()
@@ -281,22 +291,29 @@
 
         @pl.when(i == first_send - 1)
         def _():
-            arrange()
+            rr[mp] = yb[mp]
 
         @pl.when(i == first_send)
         def _():
             a2a(z * 2 + o).start()
+            for cc in (0, 1):
+                leg_one(cc).start()
+
+        @pl.when(i == nh - 1)
+        def _():
+            for cc in (0, 1):
+                await_leg(cc)
+                leg_two(cc).start()
 
         @pl.when(jnp.logical_and(i >= first_send, i < nh))
         def _():
             for e in (0, 1):
                 apart = nh - 2 * (i - first_send) - e
-                for cc in (0, 1):
-                    a2a(wrap(z + apart, nz) * 2 + cc).start()
 
                 @pl.when(apart < nh)
                 def _():
                     for cc in (0, 1):
+                        a2a(wrap(z + apart, nz) * 2 + cc).start()
                         a2a(wrap(z - apart, nz) * 2 + cc).start()
 
         return carry
@@ -331,7 +348,22 @@
     p_col = lax.broadcasted_iota(jnp.int32, (rows, 256), 1)
     p_lane = (jnp.bitwise_and(p_row, 7) - 1) * 32 + lax.shift_right_logical(p_row, 3)
     place = (p_lane == p_col).astype(F32).astype(BF16)
-    inp[...] = dot_t(place, rr[...].reshape(n_mp * fsize, 256))
+
+    def place_rows(k, carry):
+        at = pl.ds(pl.multiple_of(k * 8, 8), 8)
+        sides = []
+        for h in range(2):
+            tiles = [
+                rr[at, l].astype(F32).reshape(64, LANES) if l < levels else jnp.zeros((64, LANES), F32)
+                for l in range(4 * h, 4 * h + 4)
+            ]
+            tiles = [t.reshape(8, 1, 8, LANES) for t in swap_blocks(tiles)]
+            sides.append(jnp.concatenate(tiles, axis=1).reshape(256, LANES))
+        block = jnp.concatenate(sides, axis=1).astype(BF16)
+        inp[:, pl.ds(pl.multiple_of(k * 256, 256), 256)] = dot_t(place, block)
+        return carry
+
+    lax.fori_loop(0, n_mp // 8, place_rows, 0)
 
     part = 64
 
@@ -393,87 +425,14 @@
     lax.fori_loop(0, 2, back, 0)
 
     inv_n = 1.0 / steps
-    n_chunks = width // 256
-
-    def late(i, carry):
-        for h in (0, 1):
-
-            @pl.when(i > 0)
-            def _():
-                g_z(0, i - 1, i - 1, h).wait_recv()
-
-                @pl.when(i < nh)
-                def _():
-                    g_z(0, i - 1, i, h).start()
-
-            @pl.when(jnp.logical_and(i > 0, i < nh))
-            def _():
-                g_z(1, i, i, h).wait_recv()
-
-                @pl.when(i < nh - 1)
-                def _():
-                    g_z(1, i, i + 1, h).start()
+
+    def sent_early(i):
+        w_z(0, i, c)(i).wait_send()
+        ring_sum(1, i).wait_send()
 
         @pl.when(i > 0)
         def _():
-            g_c(0, i - 1, c).start()
-
-        @pl.when(i < nh)
-        def _():
-            g_c(1, i, c).start()
-
-        @pl.when(i < n_chunks)
-        def _():
-            at = pl.ds(pl.multiple_of(i * 256, 256), 256)
-            out[:, at] = (inp[:, at] + dot(hid[...], wall[2, :, at])).astype(BF16)
-
-        return carry
-
-    lax.fori_loop(0, nh + 1, late, 0)
-
-    def await_g(k, carry):
-        for d in (0, 1):
-            g_c(d, k, o).wait_recv()
-        return carry
-
-    lax.fori_loop(0, nh, await_g, 0)
-
-    cols = width // n_dp
-    cg_s[...] = (dot(temporal_t[...], cback[...]) * inv_n).T.astype(BF16)
-
-    def cg(target):
-        block = cg_s.at[pl.ds(pl.multiple_of(target * cols, 16), cols), :]
-        return copy_to(block, cg_r.at[dp], dp_s.at[target], dp_r.at[dp], (target, mp))
-
-    def send_cg(k, carry):
-        cg(lax.rem(dp + k, n_dp)).start()
-        return carry
-
-    lax.fori_loop(1, n_dp, send_cg, 0)
-    cg_r[dp] = cg_s[pl.ds(pl.multiple_of(dp * cols, 16), cols), :]
-
-    def tgrad(k, carry):
-        at = pl.ds(pl.multiple_of(k * chunk, chunk), chunk)
-        temporal_grad[at, :] = dot_t(cback[at, :], ctx_weight[...]).astype(BF16)
-        return carry
-
-    lax.fori_loop(0, steps // chunk, tgrad, 0)
-
-    ex_t.wait_send()
-    ex_w.wait_send()
-    copy_to(ctx_s, ctx.at[:, pl.ds(half_lane, half)], ex_s.at[2], ex_r.at[2], other).wait_send()
-
-    def sent(i, carry):
-        w_z(0, i, c)(i).wait_send()
-        for h in (0, 1):
-            g_z(0, i, i, h).wait_send()
-        ring_sum(1, i).wait_send()
-
-        @pl.when(i > 0)
-        def _():
             w_z(1, i, c)(i).wait_send()
-            for h in (0, 1):
-                g_z(1, i, i, h).wait_send()
 
         @pl.when(i < nh - 1)
         def _():
@@ -485,16 +444,102 @@
             w_x2(d, i).wait_send()
             w_y(d, i).wait_send()
             w_c(d, i, c).wait_send()
+
+        def sent_a2a(k, carry):
+            a2a(lax.rem(mp + k, n_mp)).wait_send()
+            return carry
+
+        lax.fori_loop(1 + 4 * i, jnp.minimum(5 + 4 * i, n_mp), sent_a2a, 0)
+
+    ex_t.wait_send()
+    ex_w.wait_send()
+    copy_to(ctx_s, ctx.at[:, pl.ds(half_lane, half)], ex_s.at[2], ex_r.at[2], other).wait_send()
+    for cc in (0, 1):
+        leg_two(cc).wait_send()
+    n_chunks = width // 256
+
+    def late(i, carry):
+        for h in (0, 1):
+
+            @pl.when(i > 0)
+            def _():
+                g_z(0, i - 1, i - 1, h).wait_recv()
+
+                @pl.when(i < nh)
+                def _():
+                    g_z(0, i - 1, i, h).start()
+
+            @pl.when(jnp.logical_and(i > 0, i < nh))
+            def _():
+                g_z(1, i, i, h).wait_recv()
+
+                @pl.when(i < nh - 1)
+                def _():
+                    g_z(1, i, i + 1, h).start()
+
+        @pl.when(i > 0)
+        def _():
+            g_c(0, i - 1, c).start()
+
+        @pl.when(i < nh)
+        def _():
+            g_c(1, i, c).start()
+
+        @pl.when(i < n_chunks)
+        def _():
+            at = pl.ds(pl.multiple_of(i * 256, 256), 256)
+            out[:, at] = (inp[:, at] + dot(hid[...], wall[2, :, at])).astype(BF16)
+
+        @pl.when(i < nh)
+        def _():
+            sent_early(i)
+
+        return carry
+
+    lax.fori_loop(0, nh + 1, late, 0)
+
+    def await_g(k, carry):
+        for d in (0, 1):
+            g_c(d, k, o).wait_recv()
+        return carry
+
+    lax.fori_loop(0, nh, await_g, 0)
+
+    cols = width // n_dp
+    cg_s[...] = (dot(temporal_t[...], cback[...]) * inv_n).T.astype(BF16)
+
+    def cg(target):
+        block = cg_s.at[pl.ds(pl.multiple_of(target * cols, 16), cols), :]
+        return copy_to(block, cg_r.at[dp], dp_s.at[target], dp_r.at[dp], (target, mp))
+
+    def send_cg(k, carry):
+        cg(lax.rem(dp + k, n_dp)).start()
+        return carry
+
+    lax.fori_loop(1, n_dp, send_cg, 0)
+    cg_r[dp] = cg_s[pl.ds(pl.multiple_of(dp * cols, 16), cols), :]
+
+    def tgrad(k, carry):
+        at = pl.ds(pl.multiple_of(k * chunk, chunk), chunk)
+        temporal_grad[at, :] = dot_t(cback[at, :], ctx_weight[...]).astype(BF16)
+        return carry
+
+    lax.fori_loop(0, steps // chunk, tgrad, 0)
+
+    def sent(i, carry):
+        for h in (0, 1):
+            g_z(0, i, i, h).wait_send()
+
+        @pl.when(i > 0)
+        def _():
+            for h in (0, 1):
+                g_z(1, i, i, h).wait_send()
+
+        for d in (0, 1):
             g_c(d, i, c).wait_send()
         return carry
 
     lax.fori_loop(0, nh, sent, 0)
-
-    def sent_a2a(k, carry):
-        a2a(lax.rem(mp + k, n_mp)).wait_send()
-        return carry
-
-    lax.fori_loop(1, n_mp, sent_a2a, 0)
 
     def await_cg(k, carry):
         source = lax.rem(dp + k, n_dp)
@@ -509,15 +554,10 @@
     context_grad[...] = total
 
 
-def hand_over(a, b, d, a_out, b_out, d_out, sems):
-    copies = [
-        pltpu.make_async_copy(src, dst, sems.at[k])
-        for k, (src, dst) in enumerate(((a, a_out), (b, b_out), (d, d_out)))
-    ]
-    for copy in copies:
-        copy.start()
-    for copy in copies:
-        copy.wait()
+def hand_over(a, b, d, a_out, b_out, d_out):
+    a_out[...] = a[...]
+    b_out[...] = b[...]
+    d_out[...] = d[...]
 
 
 def per_device(
@@ -531,7 +571,7 @@
     nh = n_mp // 4
     cols = width // n_dp
     half = width // 2
-    fsize = code_tables.shape[2]
+    inputs_levels = code_tables.shape[0]
     vmem = pl.BlockSpec(memory_space=pltpu.VMEM)
     dma = lambda n: pltpu.SemaphoreType.DMA((n,))
     scratch = [
@@ -541,9 +581,9 @@
         pltpu.VMEM((steps, half), F32),
         pltpu.VMEM((2 * nh, 2 * sdev, half), BF16),
         pltpu.VMEM((2 * nh, 2 * sdev, half), BF16),
-        pltpu.VMEM((fsize * n_mp // 4, 8 * LANES), BF16),
-        pltpu.VMEM((n_mp, fsize, 256), BF16),
-        pltpu.VMEM((n_mp, fsize, 256), BF16),
+        pltpu.VMEM((n_mp, inputs_levels, 8, LANES), BF16),
+        pltpu.VMEM((n_mp, inputs_levels, 8, LANES), BF16),
+        pltpu.VMEM((2, inputs_levels, 8, LANES), BF16),
         pltpu.VMEM((sdev, width), F32),
         pltpu.VMEM((sdev, half), F32),
         pltpu.VMEM((feat, steps), BF16),
@@ -558,7 +598,7 @@
         pltpu.VMEM((width, feat), BF16),
         pltpu.VMEM((n_dp, cols, feat), BF16),
     ]
-    sems = [2 * nh, 4 * nh, 2 * nh, 2 * nh, 2 * nh, 2 * nh, n_mp, 4 * nh, 2 * nh, n_dp, 3]
+    sems = [2 * nh, 4 * nh, 2 * nh, 2 * nh, 2 * nh, 2 * nh, n_mp, 4 * nh, 2 * nh, n_dp, 3, 2]
     for n in sems:
         scratch += [dma(n), dma(n)]
     out, tgrad, cgrad = pl.pallas_call(
@@ -588,13 +628,11 @@
         down_proj,
         out_grad.reshape(rows, width),
     )
-    anywhere = pl.BlockSpec(memory_space=pl.ANY)
     out, tgrad, cgrad = pl.pallas_call(
         hand_over,
         out_shape=tuple(jax.ShapeDtypeStruct(v.shape, v.dtype) for v in (out, tgrad, cgrad)),
-        in_specs=[anywhere] * 3,
-        out_specs=(anywhere,) * 3,
-        scratch_shapes=[dma(3)],
+        in_specs=[vmem] * 3,
+        out_specs=(vmem,) * 3,
         name="hand_over",
     )(out, tgrad, cgrad)
     return out.reshape(sdev, levels, width), tgrad, cgrad.T

time: 153 us -> 128 us (0.84)
  Pallas kernels: 152 us -> 127 us
    pallas_call x1, Pallas kernels: 25.9 us -> 2.03 us  [per_device(): pl.pallas_call(hand_over, out_shape=tuple((jax.ShapeDtypeStruct(v.shape,...]
where the time goes in v3:
time: 128 us
  Pallas kernels  127 us (99%)
    pallas_call x1, Pallas kernels, per_device(): pl.pallas_call(functools.partial(kernel, n_dp, n_mp), out_shape=(jax.Shap...  125 us

profile of v3, /device:TPU:1, one launch (start us, length us, event | category | flops | bytes accessed | tf_op | source)
XLA Modules:
  0.0 128.1 jit_solution(11527948110108796799)
XLA Ops:
  0.6 125.4 %depth_block.1 = (bf16[256,1024]{1,0:T(8,128)(2,1)}, bf16[1024,128]{1,0:T(8,128)(2,1)}, f32[64,128]{1,0:T(8,128)}) custom-call(bf16[1024,128]{1,0:T(8,128)(2,1)} %temporal.1, s32[7,1024]{1,0:T(8,128)} %bitcast.12, bf16[128,1024]{1,0:T(8,128)(2,1)} %ctx_weight.1, bf16[7,32,2048]{2,1,0:T(8,128)(2,1)} %bitcast.7, bf16[48,1024]{1,0:T(8,128)(2,1)} %bitcast.10, ...), custom_call_target="tpu_custom_call" | custom-call | flops 5637144576 | bytes 4194304 | tf_op jit(solution)/shard_map/depth_block/pallas_call | solution.py:604
  126.1 2.0 %hand_over.1 = (bf16[256,1024]{1,0:T(8,128)(2,1)}, bf16[1024,128]{1,0:T(8,128)(2,1)}, f32[64,128]{1,0:T(8,128)}) custom-call(bf16[256,1024]{1,0:T(8,128)(2,1)} %get-tuple-element.9.a, bf16[1024,128]{1,0:T(8,128)(2,1)} %get-tuple-element.10.b, f32[64,128]{1,0:T(8,128)} %get-tuple-element.11.d), custom_call_target="tpu_custom_call" | custom-call | tf_op jit(solution)/shard_map/hand_over/pallas_call | solution.py:631

commit v4 on v3

--- a/solution.py
+++ b/solution.py
@@ -179,7 +179,6 @@
     def await_leg(cc):
         copy_to(relay.at[cc], relay.at[cc], rl_s.at[cc], rl_r.at[cc], other).wait_recv()
 
-    temporal_t[...] = temporal[...].astype(F32).T.astype(BF16)
     ex_t.wait_recv()
     ex_w.wait_recv()
     chunk = min(256, steps)
@@ -225,6 +224,7 @@
         return copy_to(block, block, c_s.at[d * nh + i], c_r.at[d * nh + i], other)
 
     first_send = nh // 2
+    lag = 2
 
     def early(i, carry):
         for d in (0, 1):
@@ -265,25 +265,25 @@
                 for side in (0, 1):
                     w_x1(d, side, i).start()
 
-        @pl.when(jnp.logical_and(i >= 1, i < nh + 1))
+        @pl.when(jnp.logical_and(i >= lag, i < nh + lag))
         def _():
             for d in (0, 1):
                 for side in (0, 1):
-                    w_x1(d, side, i - 1).wait_recv()
+                    w_x1(d, side, i - lag).wait_recv()
             for d in (0, 1):
-                w_x2(d, i - 1).start()
-
-        @pl.when(jnp.logical_and(i >= 2, i < nh + 2))
+                w_x2(d, i - lag).start()
+
+        @pl.when(jnp.logical_and(i >= 2 * lag, i < nh + 2 * lag))
         def _():
             for d in (0, 1):
-                w_x2(d, i - 2).wait_recv()
-                w_y(d, i - 2).start()
-
-        @pl.when(i >= 3)
+                w_x2(d, i - 2 * lag).wait_recv()
+                w_y(d, i - 2 * lag).start()
+
+        @pl.when(i >= 3 * lag)
         def _():
             for d in (0, 1):
-                w_y(d, i - 3).wait_recv()
-                w_c(d, i - 3, c).start()
+                w_y(d, i - 3 * lag).wait_recv()
+                w_c(d, i - 3 * lag, c).start()
 
         @pl.when(i < first_send)
         def _():
@@ -298,6 +298,7 @@
             a2a(z * 2 + o).start()
             for cc in (0, 1):
                 leg_one(cc).start()
+            temporal_t[...] = temporal[...].astype(F32).T.astype(BF16)
 
         @pl.when(i == nh - 1)
         def _():
@@ -318,23 +319,24 @@
 
         return carry
 
-    lax.fori_loop(0, nh + 3, early, 0)
+    lax.fori_loop(0, nh + 3 * lag, early, 0)
 
     def await_w(k, carry):
         for d in (0, 1):
             w_c(d, k, o).wait_recv()
         return carry
 
-    lax.fori_loop(0, nh, await_w, 0)
-
-    fchunk = 256 if ff % 256 == 0 else 128
+    fchunk = 256 if ff % 512 == 0 else 128
+    near = ff // fchunk // 2
 
     def hidden_back(k, carry):
         at = pl.ds(pl.multiple_of(k * fchunk, fchunk), fchunk)
         hback[:, at] = dot_t(out_grad[...], wall[2, at, :])
         return carry
 
-    lax.fori_loop(0, ff // fchunk, hidden_back, 0)
+    lax.fori_loop(c * near, c * near + near, hidden_back, 0)
+    lax.fori_loop(0, nh, await_w, 0)
+    lax.fori_loop(o * near, o * near + near, hidden_back, 0)
 
     def await_a2a(k, carry):
         copy_to(yb.at[k], rr.at[k], a2a_s.at[k], a2a_r.at[k], other).wait_recv()

time: 128 us -> 127 us (level)
    pallas_call x1, Pallas kernels: 125 us -> 124 us  [per_device(): pl.pallas_call(functools.partial(kernel, n_dp, n_mp), out_shape=(jax.Shap...]
where the time goes in v4:
time: 127 us
  Pallas kernels  126 us (99%)
    pallas_call x1, Pallas kernels, per_device(): pl.pallas_call(functools.partial(kernel, n_dp, n_mp), out_shape=(jax.Shap...  124 us

profile of v4, /device:TPU:1, one launch (start us, length us, event | category | flops | bytes accessed | tf_op | source)
XLA Modules:
  0.0 126.7 jit_solution(9432594897202344648)
XLA Ops:
  0.6 124.1 %depth_block.1 = (bf16[256,1024]{1,0:T(8,128)(2,1)}, bf16[1024,128]{1,0:T(8,128)(2,1)}, f32[64,128]{1,0:T(8,128)}) custom-call(bf16[1024,128]{1,0:T(8,128)(2,1)} %temporal.1, s32[7,1024]{1,0:T(8,128)} %bitcast.12, bf16[128,1024]{1,0:T(8,128)(2,1)} %ctx_weight.1, bf16[7,32,2048]{2,1,0:T(8,128)(2,1)} %bitcast.7, bf16[48,1024]{1,0:T(8,128)(2,1)} %bitcast.10, ...), custom_call_target="tpu_custom_call" | custom-call | flops 5637144576 | bytes 4194304 | tf_op jit(solution)/shard_map/depth_block/pallas_call | solution.py:606
  124.7 2.0 %hand_over.1 = (bf16[256,1024]{1,0:T(8,128)(2,1)}, bf16[1024,128]{1,0:T(8,128)(2,1)}, f32[64,128]{1,0:T(8,128)}) custom-call(bf16[256,1024]{1,0:T(8,128)(2,1)} %get-tuple-element.9.a, bf16[1024,128]{1,0:T(8,128)(2,1)} %get-tuple-element.10.b, f32[64,128]{1,0:T(8,128)} %get-tuple-element.11.d), custom_call_target="tpu_custom_call" | custom-call | tf_op jit(solution)/shard_map/hand_over/pallas_call | solution.py:633

commit v5 on v4

--- a/solution.py
+++ b/solution.py
@@ -384,8 +384,10 @@
 
     lax.fori_loop(0, rows // part, normalise, 0)
 
+    wide = 512 if ff % 512 == 0 else fchunk
+
     def depth(k, carry):
-        at = pl.ds(pl.multiple_of(k * fchunk, fchunk), fchunk)
+        at = pl.ds(pl.multiple_of(k * wide, wide), wide)
         gate = dot_t(nlow[...], wall[0, at, :])
         upper = dot_t(nlow[...], wall[1, at, :])
         hgrad = hback[:, at]
@@ -397,7 +399,7 @@
         ngrad[...] += dot(ggrad, wall[0, at, :]) + dot(ugrad, wall[1, at, :])
         return carry
 
-    lax.fori_loop(0, ff // fchunk, depth, 0)
+    lax.fori_loop(0, ff // wide, depth, 0)
 
     part_g = sdev // 2
 

time: 127 us -> 126 us (level)
  no operation moved by 1% of the time
where the time goes in v5:
time: 126 us
  Pallas kernels  125 us (99%)
    pallas_call x1, Pallas kernels, per_device(): pl.pallas_call(functools.partial(kernel, n_dp, n_mp), out_shape=(jax.Shap...  123 us

profile of v5, /device:TPU:1, one launch (start us, length us, event | category | flops | bytes accessed | tf_op | source)
XLA Modules:
  0.0 125.9 jit_solution(9961828528471066604)
XLA Ops:
  0.6 123.2 %depth_block.1 = (bf16[256,1024]{1,0:T(8,128)(2,1)}, bf16[1024,128]{1,0:T(8,128)(2,1)}, f32[64,128]{1,0:T(8,128)}) custom-call(bf16[1024,128]{1,0:T(8,128)(2,1)} %temporal.1, s32[7,1024]{1,0:T(8,128)} %bitcast.12, bf16[128,1024]{1,0:T(8,128)(2,1)} %ctx_weight.1, bf16[7,32,2048]{2,1,0:T(8,128)(2,1)} %bitcast.7, bf16[48,1024]{1,0:T(8,128)(2,1)} %bitcast.10, ...), custom_call_target="tpu_custom_call" | custom-call | flops 5637144576 | bytes 4194304 | tf_op jit(solution)/shard_map/depth_block/pallas_call | solution.py:608
  123.9 2.0 %hand_over.1 = (bf16[256,1024]{1,0:T(8,128)(2,1)}, bf16[1024,128]{1,0:T(8,128)(2,1)}, f32[64,128]{1,0:T(8,128)}) custom-call(bf16[256,1024]{1,0:T(8,128)(2,1)} %get-tuple-element.9.a, bf16[1024,128]{1,0:T(8,128)(2,1)} %get-tuple-element.10.b, f32[64,128]{1,0:T(8,128)} %get-tuple-element.11.d), custom_call_target="tpu_custom_call" | custom-call | tf_op jit(solution)/shard_map/hand_over/pallas_call | solution.py:635
